TPU v7x, 32 devices: a whole 2x2x4 slice. The times are simulated.
32 devices in a mesh: lev: 4 (over y, x), wave: 8 (over z, core).
Axes of the slice: x: 2, y: 2, z: 4, core: 2. Of those that a mesh axis runs over, the one named last changes fastest.
Arguments:
- spectral: bfloat16 [128, 64, 3, 2, 64], P('lev', 'wave'), may hold values from -6 to 6
- modes_in: bfloat16 [128, 128], replicated, may hold values from -0.5 to 0.5
- modes_out: bfloat16 [128, 128], replicated, may hold values from -0.5 to 0.5
- mode_depth: float32 [128], replicated, may hold values from 0.1 to 10
- legendre: bfloat16 [64, 64, 32], P('wave'), may hold values from -0.75 to 0.75
- wave_map: int32 [64], replicated, may hold values from 0 to 63, as said below
- row_points: int32 [32], P('wave'), may hold values from 320 to 1280, as said below
Outputs:
- advected: float32 [3, 128, 32, 1280], P(None, 'lev', 'wave')
Inputs may be any that keep to these rules, and one draw needn't show every extreme that they name: `wave_map`: a permutation of 0 to 63; the entries at slots 2 k and 2 k + 1 add up to 63. `row_points`: some row has all 1280 points.
All inputs are finite; a program needn't handle non-finite values.
Results may differ from a plain program's by a relative error of at most 0.0059.
Values may be sent and summed in bfloat16 or wider, within the bound.
A program may use at most 64 MiB of HBM per device.

v0:
```python
import math

import jax
import jax.numpy as jnp
from jax import lax
from jax.sharding import PartitionSpec as P

LON = 1280


time_step = 0.8


def with_halo(value, sides, width):
    for axis, dim in sides:
        size, length = (lax.axis_size(axis), value.shape[dim])
        up = [(i, (i + 1) % size) for i in range(size - 1)]
        down = [(j, i) for i, j in up]
        last = lax.slice_in_dim(value, length - width, length, axis=dim)
        leading = lax.slice_in_dim(value, 0, width, axis=dim)
        before = lax.ppermute(last, axis, up)
        after = lax.ppermute(leading, axis, down)
        value = jnp.concatenate([before, value, after], axis=dim)
    return value


def damping(mode_depth, degree_of, degree_total):
    ratio = degree_of * (degree_of + 1.0) / float(degree_total * degree_total)
    return 1.0 / (1.0 + mode_depth[:, None] * ratio[None, :])


def trig_table(wave_map, lon_count):
    column = jnp.arange(lon_count, dtype=jnp.int32)
    product = wave_map[:, None] * column[None, :] % lon_count
    angles = product.astype(jnp.float32) * (2.0 * math.pi / lon_count)
    return jnp.stack([jnp.cos(angles), -jnp.sin(angles)], axis=1).astype(jnp.bfloat16)


def tendency(fields_ext):
    center = fields_ext[..., 1:-1, :]
    ahead_lon = jnp.roll(center, -1, axis=-1)
    behind_lon = jnp.roll(center, 1, axis=-1)
    ahead_lat = fields_ext[..., 2:, :]
    behind_lat = fields_ext[..., :-2, :]
    return center[0] * (ahead_lon - behind_lon) * 0.5 + center[1] * (ahead_lat - behind_lat) * 0.5


def legendre_rows(solved, legendre):
    band_rows = jnp.einsum(
        "lsfcn,snt->tlsfc", solved, legendre, preferred_element_type=jnp.float32
    ).astype(jnp.bfloat16)
    return band_rows.reshape(band_rows.shape[0], -1)


def per_device(spectral, modes_in, modes_out, mode_depth, legendre, wave_map, row_points):
    lev_rows = spectral.shape[0]
    wave_slots = spectral.shape[1]
    field_count = spectral.shape[2]
    degree_count = spectral.shape[4]
    shard_count = lax.axis_size("wave")
    first_slot = lax.axis_index("wave") * wave_slots
    local_waves = lax.dynamic_slice_in_dim(wave_map, first_slot, wave_slots)
    degrees = jnp.arange(degree_count, dtype=jnp.int32)
    keep_mask = degrees[None, :] >= local_waves[:, None]
    masked = jnp.where(keep_mask[None, :, None, None, :], spectral, jnp.zeros_like(spectral))
    flattened = masked.reshape(lev_rows, -1)
    trig_rows = trig_table(wave_map, LON).reshape(shard_count, wave_slots, 2, LON)
    norm_factor = 1.0 / math.sqrt(wave_map.shape[0])
    modal_part = jnp.dot(
        modes_in,
        lax.all_gather(flattened, "lev", axis=0, tiled=True),
        preferred_element_type=jnp.float32,
    )
    degree_of = (jnp.arange(flattened.shape[1], dtype=jnp.int32) % degree_count).astype(jnp.float32)
    scaled = (modal_part * damping(mode_depth, degree_of, degree_count)).astype(jnp.bfloat16)
    own_rows = lax.dynamic_slice_in_dim(modes_out, lax.axis_index("lev") * lev_rows, lev_rows, 0)
    solved = jnp.dot(own_rows, scaled, preferred_element_type=jnp.float32).astype(jnp.bfloat16)
    band_rows = legendre_rows(solved.reshape(spectral.shape), legendre)
    regrouped = lax.all_to_all(band_rows, "wave", split_axis=0, concat_axis=1, tiled=True)
    lat_rows = regrouped.shape[0]
    split_bands = regrouped.reshape(lat_rows, shard_count, lev_rows, wave_slots, field_count, 2)
    grid_field = (
        jnp.einsum("twlsfc,wscx->fltx", split_bands, trig_rows, preferred_element_type=jnp.float32)
        * norm_factor
    )
    wide_rows = with_halo(grid_field, (("wave", 2),), 2)
    section_wide = wide_rows[:, :, 1:-1, :] - time_step * tendency(wide_rows)
    second = 0.5 * (grid_field + section_wide[:, :, 1:-1, :] - time_step * tendency(section_wide))
    points = jnp.arange(LON, dtype=jnp.int32)[None, :] < row_points[:, None]
    return jnp.where(points[None, None, :, :], second, jnp.zeros_like(second))


def solution(mesh):
    in_specs = (
        P("lev", "wave", None, None, None),
        P(),
        P(),
        P(),
        P("wave", None, None),
        P(),
        P("wave"),
    )
    out_specs = P(None, "lev", "wave", None)
    return jax.shard_map(
        per_device, mesh=mesh, in_specs=in_specs, out_specs=out_specs, check_vma=False
    )
```

profile of v0, /device:TPU:1, one launch (start us, length us, event | category | flops | bytes accessed | tf_op | source)
XLA Modules:
  0.0 64.0 jit_solution(16339316871751392366)
XLA Ops:
  0.0 0.0 copy-start
  0.0 0.0 copy-start.4
  0.0 0.0 copy-start.3
  0.0 0.8 %dynamic_slice.7 = s32[8]{0:T(128)S(1)} dynamic-slice(s32[64]{0:T(128)} %param.12, s32[]{:T(128)S(6)} %select_n.46), dynamic_slice_sizes={8} | dynamic-slice | bytes 68 | tf_op jit(solution)/shard_map/dynamic_slice | solution.py:62
  0.8 0.1 iota_compare_fusion.1
  0.9 1.3 %broadcast_select_fusion = bf16[32,8,3,2,64]{4,3,2,1,0:T(2,128)(2,1)S(1)} fusion(bf16[32,8,3,2,64]{4,3,2,1,0:T(2,128)(2,1)} %param.7, pred[8,64]{1,0:T(8,128)(4,1)S(1)} %iota_compare_fusion.1), kind=kLoop, calls=%fused_computation.39 | loop fusion | flops 98304 | bytes 393728 | tf_op jit(solution)/shard_map/jit(_where)/select_n | solution.py:65
  2.2 0.3 reshape.139
  2.5 10.2 %all_gather.3 = bf16[128,3072]{1,0:T(8,128)(2,1)S(1)} all-gather(bf16[32,3072]{1,0:T(8,128)(2,1)S(1)} %reshape.139), channel_id=1, replica_groups=mesh['lev'=4,'wave'=8] {'lev'}, dimensions={0}, use_global_device_ids=true | all-gather | bytes 983040 | tf_op jit(solution)/shard_map/all_gather | solution.py:71
  12.7 0.0 copy-done.4
  12.7 0.0 copy-done.3
  12.7 1.5 %convolution_convert_fusion = bf16[32,3072]{1,0:T(8,128)(2,1)S(1)} fusion(bf16[128,3072]{1,0:T(8,128)(2,1)S(1)} %all_gather.3, bf16[128,128]{1,0:T(8,128)(2,1)S(1)} %copy-done.3, f32[3072]{0:T(1024)S(1)} %fusion.34, f32[128]{0:T(128)S(1)} %copy-done.4, bf16[128,128]{1,0:T(8,128)(2,1)} %param.9, s32[]{:T(128)S(6)} %select_n.45), kind=kOutput, calls=%fused_computation.4 | convolution fusion | flops 127893504 | bytes 1036804 | tf_op jit(solution)/shard_map/dot_general | solution.py:77
  14.2 0.3 reshape.140
  14.5 0.0 copy-done
  14.6 0.3 fusion.20
  14.8 1.0 %copy.19 = bf16[32,32,8,3,2]{0,4,3,2,1:T(2,128)(2,1)} copy(bf16[32,32,8,3,2]{0,1,4,3,2:T(8,128)(2,1)S(1)} %fusion.20) | data formatting | bytes 196608 | tf_op jit(solution)/shard_map/convert_element_type | solution.py:51
  15.9 3.7 %all_to_all.12 = bf16[8,4,1536]{1,0,2:T(8,128)(2,1)S(1)} reshape(bf16[32,32,8,3,2]{0,4,3,2,1:T(2,128)(2,1)} %copy.19) | data formatting | bytes 196608 | tf_op jit(solution)/shard_map/all_to_all | solution.py:79
  19.6 0.0 copy-start.1
  19.6 2.8 %copy.20 = bf16[8,4,1536]{2,1,0:T(4,128)(2,1)} copy(bf16[8,4,1536]{1,0,2:T(8,128)(2,1)S(1)} %all_to_all.12) | data formatting | bytes 196608 | tf_op jit(solution)/shard_map/all_to_all | solution.py:79
  22.4 7.3 %all-to-all-start = ((bf16[8,4,1536]{2,1,0:T(4,128)(2,1)}), bf16[8,4,1536]{2,1,0:T(4,128)(2,1)S(1)}, u32[]{:S(2)}, u32[]{:S(2)}) async-start(bf16[8,4,1536]{2,1,0:T(4,128)(2,1)} %copy.20), calls=%async_computation | async-start | bytes 196608 | tf_op jit(solution)/shard_map/all_to_all | solution.py:79
  29.7 0.0 copy-done.1
  29.7 0.1 mul.148
  29.8 0.1 copy.17
  29.9 1.5 %cosine_convert_fusion = (bf16[8,8,1,1280]{3,0,1,2:T(8,128)(2,1)S(1)}, bf16[8,8,1,1280]{3,0,1,2:T(8,128)(2,1)S(1)}) fusion(s32[8,8]{0,1:T(8,128)S(1)} %copy.17), kind=kLoop, calls=%fused_computation.50 | loop fusion | flops 983040 | bytes 327936 | tf_op jit(solution)/shard_map/convert
  31.4 3.8 %all-to-all-done = bf16[8,4,1536]{2,1,0:T(4,128)(2,1)S(1)} async-done(((bf16[8,4,1536]{2,1,0:T(4,128)(2,1)}), bf16[8,4,1536]{2,1,0:T(4,128)(2,1)S(1)}, u32[]{:S(2)}, u32[]{:S(2)}) %all-to-all-start) | async-done | bytes 98336 | tf_op jit(solution)/shard_map/all_to_all | solution.py:79
  35.2 0.8 %copy.21 = bf16[4,8,1536]{1,2,0:T(8,128)(2,1)S(1)} copy(bf16[4,8,1536]{2,0,1:T(4,128)(2,1)S(1)} %bitcast.45) | data formatting | bytes 196608 | tf_op jit(solution)/shard_map/all_to_all | solution.py:79
  36.0 0.9 %fusion.3 = f32[3,32,4,1280]{3,1,0,2:T(8,128)S(1)} fusion(bf16[4,8,32,8,3,2]{1,5,4,3,2,0:T(2,128)(2,1)S(1)} %bitcast.44, bf16[8,8,1,1280]{3,0,1,2:T(8,128)(2,1)S(1)} %get-tuple-element.18, bf16[8,8,1,1280]{3,0,1,2:T(8,128)(2,1)S(1)} %get-tuple-element.17), kind=kOutput, calls=%fused_computation.7 | convolution fusion | flops 126976000 | bytes 2392064 | tf_op jit(solution)/shard_map/twlsfc,wscx->fltx/dot_general | solution.py:83
  36.9 0.0 copy-start.2
  36.9 0.1 fusion.45
  37.1 3.2 %collective-permute-start = (f32[3,32,2,1280]{3,1,0,2:T(8,128)S(1)}, f32[3,32,2,1280]{3,1,0,2:T(8,128)S(1)}, u32[]{:S(2)}, u32[]{:S(2)}) collective-permute-start(f32[3,32,2,1280]{3,1,0,2:T(8,128)S(1)} %get-tuple-element.15), channel_id=1, source_target_pairs={{0,1},{1,2},{2,3},{3,4},{4,5},{5,6},{6,7},{8,9},{9,10},{10,11},{11... | collective-permute-start | bytes 2949128 | tf_op jit(solution)/shard_map/ppermute | solution.py:21
  40.3 2.1 %collective-permute-start.1 = (f32[3,32,2,1280]{3,1,0,2:T(8,128)S(1)}, f32[3,32,2,1280]{3,1,0,2:T(8,128)S(1)}, u32[]{:S(2)}, u32[]{:S(2)}) collective-permute-start(f32[3,32,2,1280]{3,1,0,2:T(8,128)S(1)} %get-tuple-element.16), channel_id=1, source_target_pairs={{1,0},{2,1},{3,2},{4,3},{5,4},{6,5},{7,6},{9,8},{10,9},{11,10},{12... | collective-permute-start | bytes 2949128 | tf_op jit(solution)/shard_map/ppermute | solution.py:22
  42.4 0.0 copy-done.2
  42.4 0.1 iota_compare_fusion
  42.5 8.8 %collective-permute-done = f32[3,32,2,1280]{3,1,0,2:T(8,128)S(1)} collective-permute-done((f32[3,32,2,1280]{3,1,0,2:T(8,128)S(1)}, f32[3,32,2,1280]{3,1,0,2:T(8,128)S(1)}, u32[]{:S(2)}, u32[]{:S(2)}) %collective-permute-start) | collective-permute-done | bytes 983072 | tf_op jit(solution)/shard_map/ppermute | solution.py:21
  51.3 4.4 %collective-permute-done.1 = f32[3,32,2,1280]{3,1,0,2:T(8,128)S(1)} collective-permute-done((f32[3,32,2,1280]{3,1,0,2:T(8,128)S(1)}, f32[3,32,2,1280]{3,1,0,2:T(8,128)S(1)}, u32[]{:S(2)}, u32[]{:S(2)}) %collective-permute-start.1) | collective-permute-done | bytes 983072 | tf_op jit(solution)/shard_map/ppermute | solution.py:22
  55.7 0.3 pad_maximum_fusion
  56.1 1.0 %fusion.42 = (f32[3,32,6,1279]{3,1,0,2:T(8,128)S(1)}, f32[3,32,6,1279]{3,1,0,2:T(8,128)S(1)}) fusion(f32[3,32,8,1280]{3,1,0,2:T(8,128)S(1)} %pad_maximum_fusion), kind=kLoop, calls=%fused_computation.70 | loop fusion | bytes 11787264 | tf_op jit(solution)/shard_map/jit(_roll_static)/slice | solution.py:42
  57.1 0.1 slice_bitcast_fusion.1
  57.3 2.2 %fusion.9 = f32[3,32,6,1280]{3,1,0,2:T(8,128)S(1)} fusion(f32[3,32,2,1280]{3,1,0,2:T(8,128)S(1)} %collective-permute-done.1, f32[3,32,4,1280]{3,1,0,2:T(8,128)S(1)} %fusion.3, f32[3,32,2,1280]{3,1,0,2:T(8,128)S(1)} %collective-permute-done, f32[3,32,8,1280]{3,1,0,2:T(8,128)S(1)} %pad_maximum_fusion, f32[3,32,6,1279]{3,1,0,2:T(8,128)S(1)} %get-tuple-element.8, ...), kind=kLoop, calls=%fused_computation.14 | loop fusion | flops 11059200 | bytes 17690112 | tf_op jit(solution)/shard_map/sub | solution.py:87
  59.5 0.7 %fusion.44 = (f32[3,32,4,1279]{3,1,0,2:T(8,128)S(1)}, f32[3,32,4,1279]{3,1,0,2:T(8,128)S(1)}) fusion(f32[3,32,6,1280]{3,1,0,2:T(8,128)S(1)} %fusion.9), kind=kLoop, calls=%fused_computation.72 | loop fusion | bytes 7858176 | tf_op jit(solution)/shard_map/jit(_roll_static)/slice | solution.py:42
  60.2 0.1 slice_bitcast_fusion.3
  60.3 0.1 fusion.43
  60.4 1.0 %fusion.17 = f32[3,32,4,1280]{3,1,0,2:T(8,128)S(1)} fusion(f32[3,32,6,1280]{3,1,0,2:T(8,128)S(1)} %fusion.9, f32[3,32,4,1280]{3,1,0,2:T(8,128)S(1)} %fusion.3, f32[3,32,4,1]{3,1,0,2:T(8,128)S(1)} %get-tuple-element.12, f32[3,32,4,1279]{3,1,0,2:T(8,128)S(1)} %get-tuple-element.14, f32[3,32,4,1279]{3,1,0,2:T(8,128)S(1)} %get-tuple-element.13, ...), kind=kLoop, calls=%fused_computation.27 | loop fusion | flops 5898240 | bytes 15078400 | tf_op jit(solution)/shard_map/jit(_where)/select_n | solution.py:90
  61.4 2.5 %copy.23 = f32[3,32,4,1280]{3,2,1,0:T(4,128)} copy(f32[3,32,4,1280]{3,1,0,2:T(8,128)S(1)} %fusion.17) | data formatting | bytes 3932160 | tf_op jit(solution)/shard_map/jit(_where)/select_n | solution.py:90
  (1 shorter events, 0.0 us)
Async XLA Ops:
  0.0 14.5 %copy-start = (bf16[8,64,32]{1,2,0:T(8,128)(2,1)S(1)}, bf16[8,64,32]{1,2,0:T(8,128)(2,1)}, u32[]{:S(2)}) copy-start(bf16[8,64,32]{1,2,0:T(8,128)(2,1)} %param.11) | copy-start | bytes 98308
  0.0 12.7 %copy-start.4 = (f32[128]{0:T(128)S(1)}, f32[128]{0:T(128)}, u32[]{:S(2)}) copy-start(f32[128]{0:T(128)} %param.10) | copy-start | bytes 1540
  0.0 12.7 %copy-start.3 = (bf16[128,128]{1,0:T(8,128)(2,1)S(1)}, bf16[128,128]{1,0:T(8,128)(2,1)}, u32[]{:S(2)}) copy-start(bf16[128,128]{1,0:T(8,128)(2,1)} %param.8) | copy-start | bytes 98308
  19.6 10.1 %copy-start.1 = (s32[64]{0:T(128)S(1)}, s32[64]{0:T(128)}, u32[]{:S(2)}) copy-start(s32[64]{0:T(128)} %param.12) | copy-start | bytes 772
  22.4 12.8 %all-to-all-start = ((bf16[8,4,1536]{2,1,0:T(4,128)(2,1)}), bf16[8,4,1536]{2,1,0:T(4,128)(2,1)S(1)}, u32[]{:S(2)}, u32[]{:S(2)}) async-start(bf16[8,4,1536]{2,1,0:T(4,128)(2,1)} %copy.20), calls=%async_computation | async-start | bytes 196608 | tf_op jit(solution)/shard_map/all_to_all | solution.py:79
  36.9 5.5 %copy-start.2 = (s32[4]{0:T(128)S(1)}, s32[4]{0:T(128)}, u32[]{:S(2)}) copy-start(s32[4]{0:T(128)} %param.13) | copy-start | bytes 52
  37.1 14.2 %collective-permute-start = (f32[3,32,2,1280]{3,1,0,2:T(8,128)S(1)}, f32[3,32,2,1280]{3,1,0,2:T(8,128)S(1)}, u32[]{:S(2)}, u32[]{:S(2)}) collective-permute-start(f32[3,32,2,1280]{3,1,0,2:T(8,128)S(1)} %get-tuple-element.15), channel_id=1, source_target_pairs={{0,1},{1,2},{2,3},{3,4},{4,5},{5,6},{6,7},{8,9},{9,10},{10,11},{11... | collective-permute-start | bytes 2949128 | tf_op jit(solution)/shard_map/ppermute | solution.py:21
  40.3 15.4 %collective-permute-start.1 = (f32[3,32,2,1280]{3,1,0,2:T(8,128)S(1)}, f32[3,32,2,1280]{3,1,0,2:T(8,128)S(1)}, u32[]{:S(2)}, u32[]{:S(2)}) collective-permute-start(f32[3,32,2,1280]{3,1,0,2:T(8,128)S(1)} %get-tuple-element.16), channel_id=1, source_target_pairs={{1,0},{2,1},{3,2},{4,3},{5,4},{6,5},{7,6},{9,8},{10,9},{11,10},{12... | collective-permute-start | bytes 2949128 | tf_op jit(solution)/shard_map/ppermute | solution.py:22
where the time goes:
time: 64.4 us; the launch traced here: 64 us
  waiting for transfers between devices  17 us (26%)
  local copies, waits for them, and re-layouts  14.6 us (23%)
  starting transfers between devices  12.7 us (20%)
  blocking collectives  10.2 us (16%)
  other arithmetic  6.61 us (10%)
  matrix products  2.67 us (4%)
    all_gather x1, blocking collectives, per_device(): lax.all_gather(flattened, 'lev', axis=0, tiled=True)  10.2 us
    ppermute x1, waiting for transfers between devices, with_halo(): before = lax.ppermute(last, axis, up)  8.82 us
    all_to_all x1, starting transfers between devices, per_device(): lax.all_to_all(band_rows, 'wave', split_axis=0, concat_axis=1, tiled=True)  7.34 us
    all_to_all x3, local copies, waits for them, and re-layouts, per_device(): lax.all_to_all(band_rows, 'wave', split_axis=0, concat_axis=1, tiled=True)  7.32 us
    ppermute x1, waiting for transfers between devices, with_halo(): after = lax.ppermute(leading, axis, down)  4.4 us
    all_to_all x1, waiting for transfers between devices, per_device(): lax.all_to_all(band_rows, 'wave', split_axis=0, concat_axis=1, tiled=True)  3.79 us
    ppermute x1, starting transfers between devices, with_halo(): before = lax.ppermute(last, axis, up)  3.21 us
    select_n x1, local copies, waits for them, and re-layouts, per_device(): return jnp.where(points[None, None, :, :], second, jnp.zeros_like(second))  2.54 us
  transfers between devices with their start and end apart: 3, of which 3 were waited for; matrix products, arithmetic and copies ran while one was open for 3% of the time, Pallas kernels for 0%

commit v1 on v0

--- a/solution.py
+++ b/solution.py
@@ -1,8 +1,11 @@
+import functools
 import math
 
 import jax
 import jax.numpy as jnp
 from jax import lax
+from jax.experimental import pallas as pl
+from jax.experimental.pallas import tpu as pltpu
 from jax.sharding import PartitionSpec as P
 
 LON = 1280
@@ -52,7 +55,7 @@
     return band_rows.reshape(band_rows.shape[0], -1)
 
 
-def per_device(spectral, modes_in, modes_out, mode_depth, legendre, wave_map, row_points):
+def general_path(spectral, modes_in, modes_out, mode_depth, legendre, wave_map, row_points):
     lev_rows = spectral.shape[0]
     wave_slots = spectral.shape[1]
     field_count = spectral.shape[2]
@@ -90,6 +93,283 @@
     return jnp.where(points[None, None, :, :], second, jnp.zeros_like(second))
 
 
+def iota(shape, dim):
+    return lax.broadcasted_iota(jnp.int32, shape, dim)
+
+
+def trig_rows_of(waves, points):
+    rows = waves.shape[0]
+    column = iota((rows, points), 1).astype(jnp.float32)
+    shift = (iota((rows, points), 0) % 2).astype(jnp.float32) * (points / 4)
+    product = waves * column + shift
+    turns = product * (1.0 / points)
+    left = product - jnp.floor(turns) * points
+    folded = 0.25 - jnp.abs(left * (1.0 / points) - 0.5)
+    angle = folded * (2.0 * math.pi)
+    square = angle * angle
+    total = jnp.full_like(angle, -1.0 / math.factorial(11))
+    for order in (9, 7, 5, 3, 1):
+        sign = 1.0 if order % 4 == 1 else -1.0
+        total = total * square + sign / math.factorial(order)
+    return -(total * angle)
+
+
+def exchange_kernel(
+    dims, x_ref, min_ref, mout_ref, depth_ref, leg_ref, wm_ref,
+    bands_ref, table_ref,
+    levels_buf, send_buf, recv_buf, wide, lhs, own_sem, lev_send, lev_recv, all_send, all_recv,
+):
+    groups, shards, slots, lev_rows, fields, degrees, lat_total, scale = dims
+    halo_rows = 8
+    lat_rows = lat_total // shards
+    part_slots = slots // groups
+    everyone = groups * shards
+    q = lax.axis_index("lev")
+    w = lax.axis_index("wave")
+    me = w * groups + q
+
+    def coords(place):
+        return (lax.rem(place, groups), lax.div(place, groups))
+
+    barrier = pltpu.get_barrier_semaphore()
+
+    def greet(step, carry):
+        place = lax.rem(me + step, everyone)
+        pl.semaphore_signal(barrier, inc=1, device_id=coords(place), device_id_type=pl.DeviceIdType.MESH)
+        return carry
+
+    lax.fori_loop(1, everyone, greet, 0)
+
+    own = pltpu.make_async_copy(x_ref.at[q], levels_buf.at[q], own_sem.at[0])
+    own.start()
+
+    total_slots = shards * slots
+    wm = wm_ref[...].astype(jnp.float32)
+    pair = 2 * degrees
+    halo_total = shards * halo_rows
+    row = iota((halo_total, lat_total), 0)
+    inner = row % halo_rows
+    lat = (row // halo_rows) * lat_rows + jnp.where(inner < halo_rows - 2, inner, inner - halo_rows)
+    pick = (lat == iota((halo_total, lat_total), 1)).astype(jnp.float32).astype(jnp.bfloat16)
+    double = (iota((degrees, pair), 0) == iota((degrees, pair), 1) % degrees)
+    double = double.astype(jnp.float32).astype(jnp.bfloat16)
+    lane = iota((halo_total, pair), 1)
+    degree = (lane % degrees).astype(jnp.float32)
+    legs = []
+    for s in range(part_slots):
+        leg = jnp.dot(leg_ref[q * part_slots + s], double, preferred_element_type=jnp.float32)
+        leg = jnp.dot(pick, leg.astype(jnp.bfloat16), preferred_element_type=jnp.float32)
+        place = w * slots + q * part_slots + s
+        chosen = iota((1, total_slots), 1) == place
+        wave = jnp.sum(jnp.where(chosen, wm, 0.0), axis=1, keepdims=True)
+        leg = jnp.where(degree >= wave, leg, 0.0)
+        both = [jnp.where(lane < degrees, leg, 0.0), jnp.where(lane >= degrees, leg, 0.0)]
+        legs.append(jnp.concatenate(both, axis=0).astype(jnp.bfloat16))
+    modes = min_ref.shape[0]
+    square = (modes, modes)
+    eye = iota(square, 0) == iota(square, 1)
+    depth = jnp.sum(jnp.where(eye, depth_ref[...], 0.0), axis=1, keepdims=True)
+    degree_row = (iota((modes, pair), 1) % degrees).astype(jnp.float32)
+    ratio = degree_row * (degree_row + 1.0) / float(degrees * degrees)
+    damp = 1.0 / (1.0 + depth * ratio)
+
+    pl.semaphore_wait(barrier, everyone - 1)
+
+    def lev_copy(step):
+        peer = lax.rem(q + step, groups)
+        return pltpu.make_async_remote_copy(
+            src_ref=x_ref.at[peer], dst_ref=levels_buf.at[q],
+            send_sem=lev_send.at[peer], recv_sem=lev_recv.at[q],
+            device_id=(peer, w), device_id_type=pl.DeviceIdType.MESH,
+        )
+
+    for step in range(1, groups):
+        lev_copy(step).start()
+
+    rows = 2 * total_slots
+    chosen = iota((rows, total_slots), 0) // 2 == iota((rows, total_slots), 1)
+    waves = jnp.sum(jnp.where(chosen, wm, 0.0), axis=1, keepdims=True)
+    table_ref[...] = (trig_rows_of(waves, table_ref.shape[1]) * scale).astype(jnp.bfloat16)
+
+    own.wait()
+    for step in range(1, groups):
+        peer = lax.rem(q + step, groups)
+        pltpu.make_async_remote_copy(
+            src_ref=x_ref.at[peer], dst_ref=levels_buf.at[peer],
+            send_sem=lev_send.at[peer], recv_sem=lev_recv.at[peer],
+            device_id=(peer, w), device_id_type=pl.DeviceIdType.MESH,
+        ).wait_recv()
+
+    columns = levels_buf.shape[2]
+    level_count = groups * lev_rows
+    coef = levels_buf[...].reshape(level_count, columns)
+    modal = jnp.dot(min_ref[...], coef, preferred_element_type=jnp.float32)
+    scaled = jnp.concatenate(
+        [modal[:, i * pair : (i + 1) * pair] * damp for i in range(columns // pair)], axis=1
+    ).astype(jnp.bfloat16)
+    solved = jnp.dot(mout_ref[...], scaled, preferred_element_type=jnp.float32).astype(jnp.bfloat16)
+    width = send_buf.shape[2]
+    spare = jnp.zeros((width - fields * lev_rows, pair), jnp.bfloat16)
+    for to in range(groups):
+        outs = []
+        for s in range(part_slots):
+            pieces = []
+            for f in range(fields):
+                at = (s * fields + f) * pair
+                pieces.append(solved[to * lev_rows : (to + 1) * lev_rows, at : at + pair])
+            stack = jnp.concatenate(pieces + [spare], axis=0)
+            outs.append(lax.dot_general(
+                legs[s], stack, (((1,), (1,)), ((), ())), preferred_element_type=jnp.float32
+            ))
+        for shard in range(shards):
+            message = []
+            for s in range(part_slots):
+                for c in range(2):
+                    at = (c * shards + shard) * halo_rows
+                    message.append(outs[s][at : at + halo_rows])
+            send_buf[shard * groups + to] = jnp.concatenate(message, axis=0).astype(jnp.bfloat16)
+
+    def all_copy(peer, land):
+        return pltpu.make_async_remote_copy(
+            src_ref=send_buf.at[peer], dst_ref=recv_buf.at[land],
+            send_sem=all_send.at[peer], recv_sem=all_recv.at[land],
+            device_id=coords(peer), device_id_type=pl.DeviceIdType.MESH,
+        )
+
+    def start(step, carry):
+        all_copy(lax.rem(me + step, everyone), me).start()
+        return carry
+
+    lax.fori_loop(1, everyone, start, 0)
+    mine = pltpu.make_async_copy(send_buf.at[me], recv_buf.at[me], own_sem.at[1])
+    mine.start()
+    mine.wait()
+
+    def finish(step, carry):
+        peer = lax.rem(me + step, everyone)
+        all_copy(peer, peer).wait_recv()
+        return carry
+
+    lax.fori_loop(1, everyone, finish, 0)
+    for t in range(0, everyone, 8):
+        part = recv_buf[t : t + 8]
+        wide[t * part.shape[1] : (t + 8) * part.shape[1]] = part.reshape(-1, width).astype(jnp.float32)
+    used = fields * lev_rows
+    for t in range(halo_rows):
+        rows_t = wide[pl.ds(t, rows, stride=halo_rows), :]
+        lhs[pl.ds(t, used, stride=halo_rows), :] = rows_t.T[:used]
+    bands_ref[...] = lhs[...].astype(jnp.bfloat16)
+
+    def sent(step, carry):
+        all_copy(lax.rem(me + step, everyone), me).wait_send()
+        return carry
+
+    lax.fori_loop(1, everyone, sent, 0)
+    for step in range(1, groups):
+        lev_copy(step).wait_send()
+
+
+def section_kernel(scale, points_ref, bands_ref, table_ref, out_ref, grid_buf):
+    fields, chunk, halo_rows, depth = bands_ref.shape
+    lat_rows, width = out_ref.shape[2], out_ref.shape[3]
+    table = table_ref[...]
+    for f in range(fields):
+        part = bands_ref[f].reshape(chunk * halo_rows, depth)
+        value = jnp.dot(part, table, preferred_element_type=jnp.float32)
+        grid_buf[f] = (value if scale is None else value * scale).reshape(chunk, halo_rows, width)
+    row = iota((halo_rows, width), 0)
+    limit = jnp.zeros((halo_rows, width), jnp.int32)
+    for t in range(lat_rows):
+        limit = jnp.where(row == t, points_ref[t], limit)
+    keep = iota((halo_rows, width), 1) < limit
+
+    def slopes(value):
+        lon = pltpu.roll(value, width - 1, 1) - pltpu.roll(value, 1, 1)
+        lat = pltpu.roll(value, halo_rows - 1, 0) - pltpu.roll(value, 1, 0)
+        return lon, lat
+
+    def level(i, carry):
+        grid = [grid_buf[f, i] for f in range(fields)]
+        east, north = grid[0] * (0.5 * time_step), grid[1] * (0.5 * time_step)
+        first = []
+        for value in grid:
+            lon, lat = slopes(value)
+            first.append(value - (east * lon + north * lat))
+        east, north = first[0] * (0.25 * time_step), first[1] * (0.25 * time_step)
+        for f in range(fields):
+            lon, lat = slopes(first[f])
+            second = 0.5 * (grid[f] + first[f]) - (east * lon + north * lat)
+            out_ref[f, i] = jnp.where(keep, second, 0.0)[:lat_rows]
+        return carry
+
+    lax.fori_loop(0, chunk, level, 0)
+
+
+def per_device(spectral, modes_in, modes_out, mode_depth, legendre, wave_map, row_points):
+    lev_rows, slots, fields, _, degrees = spectral.shape
+    groups, shards = lax.axis_size("lev"), lax.axis_size("wave")
+    lat_total = legendre.shape[2]
+    lat_rows = lat_total // shards
+    used = fields * lev_rows
+    fits = slots % groups == 0 and 2 * degrees == 128 and lat_rows == 4 and used <= 128
+    fits = fits and lev_rows % 16 == 0 and (groups * shards) % 8 == 0 and 2 * shards * slots == 128
+    if not fits:
+        return general_path(spectral, modes_in, modes_out, mode_depth, legendre, wave_map, row_points)
+    everyone, halo_rows, width = groups * shards, 8, 128
+    part_slots = slots // groups
+    rows = 2 * shards * slots
+    norm = 1.0 / math.sqrt(shards * slots)
+    exact = math.frexp(norm)[0] == 0.5
+    columns = part_slots * fields * 2 * degrees
+    x = spectral.reshape(lev_rows, groups, columns).transpose(1, 0, 2)
+    dims = (groups, shards, slots, lev_rows, fields, degrees, lat_total, norm if exact else 1.0)
+    vmem = pl.BlockSpec(memory_space=pltpu.VMEM)
+    message = part_slots * 2 * halo_rows
+    bands, table = pl.pallas_call(
+        functools.partial(exchange_kernel, dims),
+        out_shape=(
+            jax.ShapeDtypeStruct((used * halo_rows, rows), jnp.bfloat16),
+            jax.ShapeDtypeStruct((rows, LON), jnp.bfloat16),
+        ),
+        in_specs=[vmem] * 6,
+        out_specs=(vmem, vmem),
+        scratch_shapes=[
+            pltpu.VMEM((groups, lev_rows, columns), jnp.bfloat16),
+            pltpu.VMEM((everyone, message, width), jnp.bfloat16),
+            pltpu.VMEM((everyone, message, width), jnp.bfloat16),
+            pltpu.VMEM((everyone * message, width), jnp.float32),
+            pltpu.VMEM((used * halo_rows, rows), jnp.float32),
+            pltpu.SemaphoreType.DMA((2,)),
+            pltpu.SemaphoreType.DMA((groups,)),
+            pltpu.SemaphoreType.DMA((groups,)),
+            pltpu.SemaphoreType.DMA((everyone,)),
+            pltpu.SemaphoreType.DMA((everyone,)),
+        ],
+        compiler_params=pltpu.CompilerParams(
+            collective_id=0, has_side_effects=True, vmem_limit_bytes=32 * 1024 * 1024
+        ),
+        name="exchange",
+    )(
+        x, modes_in, modes_out, mode_depth.reshape(1, -1),
+        jnp.swapaxes(legendre, 1, 2), wave_map.reshape(1, -1),
+    )
+    chunk = 8
+    return pl.pallas_call(
+        functools.partial(section_kernel, None if exact else norm),
+        grid=(lev_rows // chunk,),
+        out_shape=jax.ShapeDtypeStruct((fields, lev_rows, lat_rows, LON), jnp.float32),
+        in_specs=[
+            pl.BlockSpec(memory_space=pltpu.SMEM),
+            pl.BlockSpec((fields, chunk, halo_rows, rows), lambda i: (0, i, 0, 0)),
+            pl.BlockSpec((rows, LON), lambda i: (0, 0)),
+        ],
+        out_specs=pl.BlockSpec((fields, chunk, lat_rows, LON), lambda i: (0, i, 0, 0)),
+        scratch_shapes=[pltpu.VMEM((fields, chunk, halo_rows, LON), jnp.float32)],
+        compiler_params=pltpu.CompilerParams(vmem_limit_bytes=32 * 1024 * 1024),
+        name="sections",
+    )(row_points, bands.reshape(fields, lev_rows, halo_rows, rows), table)
+
+
 def solution(mesh):
     in_specs = (
         P("lev", "wave", None, None, None),

time: 64.4 us -> 34.3 us (0.53)
  the two profiles are of different devices: /device:TPU:1 before, /device:TPU:0 now
where the time goes in v1:
time: 34.3 us; the launch traced here: 33.9 us
  Pallas kernels  28.2 us (82%)
  local copies, waits for them, and re-layouts  5.6 us (16%)
    pallas_call x1, Pallas kernels, per_device(): pl.pallas_call(functools.partial(exchange_kernel, dims), out_shape=(jax.S...  18.3 us
    pallas_call x1, Pallas kernels, per_device(): pl.pallas_call(functools.partial(section_kernel, None if exact else norm)...  9.95 us
    unnamed x12, local copies, waits for them, and re-layouts  4.31 us
    reshape x2, local copies, waits for them, and re-layouts, per_device(): x = spectral.reshape(lev_rows, groups, columns).transpose(1, 0, 2)  1.29 us

profile of v1, /device:TPU:0, one launch (start us, length us, event | category | flops | bytes accessed | tf_op | source)
XLA Modules:
  0.0 33.9 jit_solution(2778451730011510223)
XLA Ops:
  0.0 1.3 %reshape.12 = bf16[32,4,768]{2,1,0:T(4,128)(2,1)S(1)} reshape(bf16[32,8,3,2,64]{4,3,2,1,0:T(2,128)(2,1)} %param.7) | data formatting | bytes 393216 | tf_op jit(solution)/shard_map/reshape | solution.py:324
  1.3 0.0 copy-start
  1.3 0.8 %copy-done = bf16[8,64,32]{1,2,0:T(8,128)(2,1)S(1)} copy-done((bf16[8,64,32]{1,2,0:T(8,128)(2,1)S(1)}, bf16[8,64,32]{1,2,0:T(8,128)(2,1)}, u32[]{:S(2)}) %copy-start) | copy-done | bytes 32792
  2.1 0.0 copy-start.1
  2.1 0.8 %copy-done.1 = bf16[128,128]{1,0:T(8,128)(2,1)S(1)} copy-done((bf16[128,128]{1,0:T(8,128)(2,1)S(1)}, bf16[128,128]{1,0:T(8,128)(2,1)}, u32[]{:S(2)}) %copy-start.1) | copy-done | bytes 32792
  2.9 0.0 copy-start.2
  2.9 0.8 %copy-done.2 = bf16[128,128]{1,0:T(8,128)(2,1)S(1)} copy-done((bf16[128,128]{1,0:T(8,128)(2,1)S(1)}, bf16[128,128]{1,0:T(8,128)(2,1)}, u32[]{:S(2)}) %copy-start.2) | copy-done | bytes 32792
  3.7 0.0 copy-start.3
  3.7 0.7 %copy-done.3 = f32[128]{0:T(128)S(1)} copy-done((f32[128]{0:T(128)S(1)}, f32[128]{0:T(128)}, u32[]{:S(2)}) %copy-start.3) | copy-done | bytes 536
  4.3 0.0 copy-start.4
  4.3 0.7 %copy-done.4 = s32[64]{0:T(128)S(1)} copy-done((s32[64]{0:T(128)S(1)}, s32[64]{0:T(128)}, u32[]{:S(2)}) %copy-start.4) | copy-done | bytes 280
  5.0 18.3 %exchange.1 = (bf16[768,128]{1,0:T(8,128)(2,1)S(1)}, bf16[128,1280]{1,0:T(8,128)(2,1)S(1)}) custom-call(bf16[4,32,768]{2,1,0:T(8,128)(2,1)S(1)} %bitcast.7, bf16[128,128]{1,0:T(8,128)(2,1)S(1)} %copy-done.1, bf16[128,128]{1,0:T(8,128)(2,1)S(1)} %copy-done.2, f32[1,128]{1,0:T(1,128)S(1)} %bitcast.10, bf16[8,32,64]{2,1,0:T(8,128)(2,1)S(1)} %bitcast.9, ...), custom_call_target="tpu_custom_call" | custom-call | tf_op jit(solution)/shard_map/exchange/pallas_call | solution.py:328
  23.3 0.0 copy-start.5
  23.3 0.6 %copy-done.5 = s32[4]{0:T(128)S(1)} copy-done((s32[4]{0:T(128)S(1)}, s32[4]{0:T(128)}, u32[]{:S(2)}) %copy-start.5) | copy-done | bytes 40
  23.9 10.0 %sections.1 = f32[3,32,4,1280]{3,2,1,0:T(4,128)} custom-call(s32[4]{0:T(128)S(1)} %copy-done.5, bf16[3,32,8,128]{3,2,1,0:T(8,128)(2,1)S(1)} %bitcast.8, bf16[128,1280]{1,0:T(8,128)(2,1)S(1)} %get-tuple-element.8.table_ref), custom_call_target="tpu_custom_call" | custom-call | tf_op jit(solution)/shard_map/sections/pallas_call | solution.py:357
  (1 shorter events, 0.0 us)
Async XLA Ops:
  1.3 0.8 %copy-start = (bf16[8,64,32]{1,2,0:T(8,128)(2,1)S(1)}, bf16[8,64,32]{1,2,0:T(8,128)(2,1)}, u32[]{:S(2)}) copy-start(bf16[8,64,32]{1,2,0:T(8,128)(2,1)} %param.11) | copy-start | bytes 98308
  2.1 0.8 %copy-start.1 = (bf16[128,128]{1,0:T(8,128)(2,1)S(1)}, bf16[128,128]{1,0:T(8,128)(2,1)}, u32[]{:S(2)}) copy-start(bf16[128,128]{1,0:T(8,128)(2,1)} %min_ref.1) | copy-start | bytes 98308
  2.9 0.8 %copy-start.2 = (bf16[128,128]{1,0:T(8,128)(2,1)S(1)}, bf16[128,128]{1,0:T(8,128)(2,1)}, u32[]{:S(2)}) copy-start(bf16[128,128]{1,0:T(8,128)(2,1)} %mout_ref.1) | copy-start | bytes 98308
  3.7 0.7 %copy-start.3 = (f32[128]{0:T(128)S(1)}, f32[128]{0:T(128)}, u32[]{:S(2)}) copy-start(f32[128]{0:T(128)} %param.10) | copy-start | bytes 1540
  4.3 0.7 %copy-start.4 = (s32[64]{0:T(128)S(1)}, s32[64]{0:T(128)}, u32[]{:S(2)}) copy-start(s32[64]{0:T(128)} %param.12) | copy-start | bytes 772
  23.3 0.7 %copy-start.5 = (s32[4]{0:T(128)S(1)}, s32[4]{0:T(128)}, u32[]{:S(2)}) copy-start(s32[4]{0:T(128)} %points_ref.1) | copy-start | bytes 52

commit v2 on v1

--- a/solution.py
+++ b/solution.py
@@ -97,11 +97,10 @@
     return lax.broadcasted_iota(jnp.int32, shape, dim)
 
 
-def trig_rows_of(waves, points):
+def trig_rows_of(waves, parts, points):
     rows = waves.shape[0]
     column = iota((rows, points), 1).astype(jnp.float32)
-    shift = (iota((rows, points), 0) % 2).astype(jnp.float32) * (points / 4)
-    product = waves * column + shift
+    product = waves * column + parts * (points / 4)
     turns = product * (1.0 / points)
     left = product - jnp.floor(turns) * points
     folded = 0.25 - jnp.abs(left * (1.0 / points) - 0.5)
@@ -115,9 +114,11 @@
 
 
 def exchange_kernel(
-    dims, x_ref, min_ref, mout_ref, depth_ref, leg_ref, wm_ref,
-    bands_ref, table_ref,
-    levels_buf, send_buf, recv_buf, wide, lhs, own_sem, lev_send, lev_recv, all_send, all_recv,
+    dims, x_ref, min_hbm, mout_hbm, depth_hbm, leg_hbm, wm_hbm, points_hbm,
+    bands_ref, table_ref, slope_ref, limit_ref,
+    min_ref, mout_ref, depth_ref, leg_ref, wm_ref, points_ref,
+    levels_buf, solved_buf, send_buf, recv_buf, wide,
+    in_sem, own_sem, lev_send, lev_recv, all_send, all_recv,
 ):
     groups, shards, slots, lev_rows, fields, degrees, lat_total, scale = dims
     halo_rows = 8
@@ -140,8 +141,30 @@
 
     lax.fori_loop(1, everyone, greet, 0)
 
+    pairs = [
+        (wm_hbm, wm_ref), (leg_hbm.at[pl.ds(q * part_slots, part_slots)], leg_ref),
+        (depth_hbm, depth_ref), (points_hbm, points_ref), (min_hbm, min_ref), (mout_hbm, mout_ref),
+    ]
+    inputs = [pltpu.make_async_copy(a, b, in_sem.at[i]) for i, (a, b) in enumerate(pairs)]
+    for copy in inputs:
+        copy.start()
     own = pltpu.make_async_copy(x_ref.at[q], levels_buf.at[q], own_sem.at[0])
     own.start()
+
+    pl.semaphore_wait(barrier, everyone - 1)
+
+    def lev_copy(step):
+        peer = lax.rem(q + step, groups)
+        return pltpu.make_async_remote_copy(
+            src_ref=x_ref.at[peer], dst_ref=levels_buf.at[q],
+            send_sem=lev_send.at[peer], recv_sem=lev_recv.at[q],
+            device_id=(peer, w), device_id_type=pl.DeviceIdType.MESH,
+        )
+
+    for step in range(1, groups):
+        lev_copy(step).start()
+    for copy in inputs:
+        copy.wait()
 
     total_slots = shards * slots
     wm = wm_ref[...].astype(jnp.float32)
@@ -153,43 +176,39 @@
     pick = (lat == iota((halo_total, lat_total), 1)).astype(jnp.float32).astype(jnp.bfloat16)
     double = (iota((degrees, pair), 0) == iota((degrees, pair), 1) % degrees)
     double = double.astype(jnp.float32).astype(jnp.bfloat16)
-    lane = iota((halo_total, pair), 1)
-    degree = (lane % degrees).astype(jnp.float32)
+    degree = (iota((halo_total, pair), 1) % degrees).astype(jnp.float32)
     legs = []
     for s in range(part_slots):
-        leg = jnp.dot(leg_ref[q * part_slots + s], double, preferred_element_type=jnp.float32)
+        leg = jnp.dot(leg_ref[s], double, preferred_element_type=jnp.float32)
         leg = jnp.dot(pick, leg.astype(jnp.bfloat16), preferred_element_type=jnp.float32)
         place = w * slots + q * part_slots + s
         chosen = iota((1, total_slots), 1) == place
         wave = jnp.sum(jnp.where(chosen, wm, 0.0), axis=1, keepdims=True)
-        leg = jnp.where(degree >= wave, leg, 0.0)
-        both = [jnp.where(lane < degrees, leg, 0.0), jnp.where(lane >= degrees, leg, 0.0)]
-        legs.append(jnp.concatenate(both, axis=0).astype(jnp.bfloat16))
+        legs.append(jnp.where(degree >= wave, leg, 0.0).astype(jnp.bfloat16))
+    legs = jnp.concatenate(legs, axis=1)
     modes = min_ref.shape[0]
-    square = (modes, modes)
-    eye = iota(square, 0) == iota(square, 1)
+    eye = iota((modes, modes), 0) == iota((modes, modes), 1)
     depth = jnp.sum(jnp.where(eye, depth_ref[...], 0.0), axis=1, keepdims=True)
     degree_row = (iota((modes, pair), 1) % degrees).astype(jnp.float32)
     ratio = degree_row * (degree_row + 1.0) / float(degrees * degrees)
     damp = 1.0 / (1.0 + depth * ratio)
 
-    pl.semaphore_wait(barrier, everyone - 1)
-
-    def lev_copy(step):
-        peer = lax.rem(q + step, groups)
-        return pltpu.make_async_remote_copy(
-            src_ref=x_ref.at[peer], dst_ref=levels_buf.at[q],
-            send_sem=lev_send.at[peer], recv_sem=lev_recv.at[q],
-            device_id=(peer, w), device_id_type=pl.DeviceIdType.MESH,
-        )
-
-    for step in range(1, groups):
-        lev_copy(step).start()
-
     rows = 2 * total_slots
-    chosen = iota((rows, total_slots), 0) // 2 == iota((rows, total_slots), 1)
-    waves = jnp.sum(jnp.where(chosen, wm, 0.0), axis=1, keepdims=True)
-    table_ref[...] = (trig_rows_of(waves, table_ref.shape[1]) * scale).astype(jnp.bfloat16)
+    row = iota((rows, total_slots), 0)
+    slot = part_slots * (row % everyone) + row // (2 * everyone)
+    waves = jnp.sum(jnp.where(slot == iota((rows, total_slots), 1), wm, 0.0), axis=1, keepdims=True)
+    parts = ((iota((rows, 1), 0) // everyone) % 2).astype(jnp.float32)
+    points = table_ref.shape[1]
+    table = (trig_rows_of(waves, parts, points) * scale).astype(jnp.bfloat16)
+    table_ref[...] = table
+    table = table.astype(jnp.float32)
+    slope = pltpu.roll(table, points - 1, 1) - pltpu.roll(table, 1, 1)
+    high = slope.astype(jnp.bfloat16)
+    slope_ref[:rows] = high
+    slope_ref[rows:] = (slope - high.astype(jnp.float32)).astype(jnp.bfloat16)
+    match = iota((limit_ref.shape[0], lat_rows), 0) == iota((limit_ref.shape[0], lat_rows), 1)
+    limit = jnp.sum(jnp.where(match, points_ref[...].astype(jnp.float32), 0.0), axis=1, keepdims=True)
+    limit_ref[...] = jnp.broadcast_to(limit, limit_ref.shape).astype(jnp.int32)
 
     own.wait()
     for step in range(1, groups):
@@ -208,26 +227,7 @@
         [modal[:, i * pair : (i + 1) * pair] * damp for i in range(columns // pair)], axis=1
     ).astype(jnp.bfloat16)
     solved = jnp.dot(mout_ref[...], scaled, preferred_element_type=jnp.float32).astype(jnp.bfloat16)
-    width = send_buf.shape[2]
-    spare = jnp.zeros((width - fields * lev_rows, pair), jnp.bfloat16)
-    for to in range(groups):
-        outs = []
-        for s in range(part_slots):
-            pieces = []
-            for f in range(fields):
-                at = (s * fields + f) * pair
-                pieces.append(solved[to * lev_rows : (to + 1) * lev_rows, at : at + pair])
-            stack = jnp.concatenate(pieces + [spare], axis=0)
-            outs.append(lax.dot_general(
-                legs[s], stack, (((1,), (1,)), ((), ())), preferred_element_type=jnp.float32
-            ))
-        for shard in range(shards):
-            message = []
-            for s in range(part_slots):
-                for c in range(2):
-                    at = (c * shards + shard) * halo_rows
-                    message.append(outs[s][at : at + halo_rows])
-            send_buf[shard * groups + to] = jnp.concatenate(message, axis=0).astype(jnp.bfloat16)
+    solved_buf[...] = solved.reshape(groups, lev_rows, columns)
 
     def all_copy(peer, land):
         return pltpu.make_async_remote_copy(
@@ -236,11 +236,34 @@
             device_id=coords(peer), device_id_type=pl.DeviceIdType.MESH,
         )
 
-    def start(step, carry):
-        all_copy(lax.rem(me + step, everyone), me).start()
-        return carry
-
-    lax.fori_loop(1, everyone, start, 0)
+    lane = iota((lev_rows, pair), 1)
+    empty = jnp.zeros((2 * lev_rows, pair), jnp.bfloat16)
+    for turn in range(groups):
+        to = lax.rem(q + 1 + turn, groups)
+        outs = []
+        for f in range(fields):
+            blocks = []
+            for s in range(part_slots):
+                at = (s * fields + f) * pair
+                tile = solved_buf[to, :, at : at + pair]
+                none = jnp.zeros_like(tile)
+                split = [jnp.where(lane < degrees, tile, none), jnp.where(lane >= degrees, tile, none)]
+                split = jnp.concatenate(split, axis=0)
+                blocks.append(jnp.concatenate([split if k == s else empty for k in range(part_slots)], axis=1))
+            outs.append(lax.dot_general(
+                legs, jnp.concatenate(blocks, axis=0), (((1,), (1,)), ((), ())),
+                preferred_element_type=jnp.float32,
+            ))
+        for shard in range(shards):
+            at = shard * halo_rows
+            message = jnp.concatenate([out[at : at + halo_rows] for out in outs], axis=0)
+            send_buf[shard * groups + to] = message.astype(jnp.bfloat16)
+
+        def start(step, carry):
+            all_copy(lax.rem(w + step, shards) * groups + to, me).start()
+            return carry
+
+        lax.fori_loop(0 if turn < groups - 1 else 1, shards, start, 0)
     mine = pltpu.make_async_copy(send_buf.at[me], recv_buf.at[me], own_sem.at[1])
     mine.start()
     mine.wait()
@@ -251,14 +274,22 @@
         return carry
 
     lax.fori_loop(1, everyone, finish, 0)
-    for t in range(0, everyone, 8):
-        part = recv_buf[t : t + 8]
-        wide[t * part.shape[1] : (t + 8) * part.shape[1]] = part.reshape(-1, width).astype(jnp.float32)
-    used = fields * lev_rows
-    for t in range(halo_rows):
-        rows_t = wide[pl.ds(t, rows, stride=halo_rows), :]
-        lhs[pl.ds(t, used, stride=halo_rows), :] = rows_t.T[:used]
-    bands_ref[...] = lhs[...].astype(jnp.bfloat16)
+    message = fields * halo_rows
+    wide[...] = recv_buf[...].reshape(everyone * message, rows).astype(jnp.float32)
+    lane = iota((lev_rows, rows), 1) // everyone
+    count = rows // everyone
+    for first in range(0, message, count):
+        stack = [wide[pl.ds(first + j, everyone, stride=message), :] for j in range(count)]
+        turned = jnp.concatenate(stack, axis=0).T
+        for j in range(count):
+            value = None
+            for g in range(count):
+                part = turned[g * lev_rows : (g + 1) * lev_rows]
+                if g != j:
+                    part = pltpu.roll(part, ((g - j) * everyone) % rows, 1)
+                value = part if value is None else jnp.where(lane == g, part, value)
+            f, t = divmod(first + j, halo_rows)
+            bands_ref[t, f] = value.astype(jnp.bfloat16)
 
     def sent(step, carry):
         all_copy(lax.rem(me + step, everyone), me).wait_send()
@@ -269,40 +300,37 @@
         lev_copy(step).wait_send()
 
 
-def section_kernel(scale, points_ref, bands_ref, table_ref, out_ref, grid_buf):
-    fields, chunk, halo_rows, depth = bands_ref.shape
+def section_kernel(scale, limit_ref, bands_ref, table_ref, slope_ref, out_ref, grid_buf, lon_buf, first_buf):
+    halo_rows, fields, chunk, depth = bands_ref.shape
     lat_rows, width = out_ref.shape[2], out_ref.shape[3]
-    table = table_ref[...]
-    for f in range(fields):
-        part = bands_ref[f].reshape(chunk * halo_rows, depth)
-        value = jnp.dot(part, table, preferred_element_type=jnp.float32)
-        grid_buf[f] = (value if scale is None else value * scale).reshape(chunk, halo_rows, width)
-    row = iota((halo_rows, width), 0)
-    limit = jnp.zeros((halo_rows, width), jnp.int32)
+    inner = [halo_rows - 1] + list(range(lat_rows + 1))
+
+    def product(a, b):
+        value = jnp.dot(a, b, preferred_element_type=jnp.float32)
+        return (value if scale is None else value * scale).reshape(fields, chunk, width)
+
+    for t in range(halo_rows):
+        part = bands_ref[t].reshape(fields * chunk, depth)
+        grid_buf[t] = product(part, table_ref[...])
+        if t in inner:
+            lon_buf[t] = product(jnp.concatenate([part, part], axis=1), slope_ref[...])
+
+    def around(ref, t, f):
+        return ref[(t + 1) % halo_rows, f] - ref[(t - 1) % halo_rows, f]
+
+    for t in inner:
+        east, north = grid_buf[t, 0] * (0.5 * time_step), grid_buf[t, 1] * (0.5 * time_step)
+        for f in range(fields):
+            first_buf[t, f] = grid_buf[t, f] - (east * lon_buf[t, f] + north * around(grid_buf, t, f))
+    column = iota((chunk, width), 1)
     for t in range(lat_rows):
-        limit = jnp.where(row == t, points_ref[t], limit)
-    keep = iota((halo_rows, width), 1) < limit
-
-    def slopes(value):
-        lon = pltpu.roll(value, width - 1, 1) - pltpu.roll(value, 1, 1)
-        lat = pltpu.roll(value, halo_rows - 1, 0) - pltpu.roll(value, 1, 0)
-        return lon, lat
-
-    def level(i, carry):
-        grid = [grid_buf[f, i] for f in range(fields)]
-        east, north = grid[0] * (0.5 * time_step), grid[1] * (0.5 * time_step)
-        first = []
-        for value in grid:
-            lon, lat = slopes(value)
-            first.append(value - (east * lon + north * lat))
-        east, north = first[0] * (0.25 * time_step), first[1] * (0.25 * time_step)
+        east, north = first_buf[t, 0] * (0.25 * time_step), first_buf[t, 1] * (0.25 * time_step)
+        keep = column < limit_ref[t : t + 1, :1]
         for f in range(fields):
-            lon, lat = slopes(first[f])
-            second = 0.5 * (grid[f] + first[f]) - (east * lon + north * lat)
-            out_ref[f, i] = jnp.where(keep, second, 0.0)[:lat_rows]
-        return carry
-
-    lax.fori_loop(0, chunk, level, 0)
+            value = first_buf[t, f]
+            lon = pltpu.roll(value, width - 1, 1) - pltpu.roll(value, 1, 1)
+            second = 0.5 * (grid_buf[t, f] + value) - (east * lon + north * around(first_buf, t, f))
+            out_ref[f, :, t, :] = jnp.where(keep, second, 0.0)
 
 
 def per_device(spectral, modes_in, modes_out, mode_depth, legendre, wave_map, row_points):
@@ -310,35 +338,46 @@
     groups, shards = lax.axis_size("lev"), lax.axis_size("wave")
     lat_total = legendre.shape[2]
     lat_rows = lat_total // shards
-    used = fields * lev_rows
-    fits = slots % groups == 0 and 2 * degrees == 128 and lat_rows == 4 and used <= 128
-    fits = fits and lev_rows % 16 == 0 and (groups * shards) % 8 == 0 and 2 * shards * slots == 128
+    everyone, halo_rows = groups * shards, 8
+    part_slots = slots // groups
+    rows = 2 * shards * slots
+    fits = slots == 2 * groups and 2 * degrees == 128 and lat_rows == 4
+    fits = fits and lev_rows == 32 and everyone == 32 and rows == 128
     if not fits:
         return general_path(spectral, modes_in, modes_out, mode_depth, legendre, wave_map, row_points)
-    everyone, halo_rows, width = groups * shards, 8, 128
-    part_slots = slots // groups
-    rows = 2 * shards * slots
     norm = 1.0 / math.sqrt(shards * slots)
     exact = math.frexp(norm)[0] == 0.5
     columns = part_slots * fields * 2 * degrees
+    modes = modes_in.shape[0]
     x = spectral.reshape(lev_rows, groups, columns).transpose(1, 0, 2)
     dims = (groups, shards, slots, lev_rows, fields, degrees, lat_total, norm if exact else 1.0)
     vmem = pl.BlockSpec(memory_space=pltpu.VMEM)
-    message = part_slots * 2 * halo_rows
-    bands, table = pl.pallas_call(
+    hbm = pl.BlockSpec(memory_space=pltpu.HBM)
+    message = fields * halo_rows
+    bf16 = jnp.bfloat16
+    bands, table, slope, limit = pl.pallas_call(
         functools.partial(exchange_kernel, dims),
         out_shape=(
-            jax.ShapeDtypeStruct((used * halo_rows, rows), jnp.bfloat16),
-            jax.ShapeDtypeStruct((rows, LON), jnp.bfloat16),
+            jax.ShapeDtypeStruct((halo_rows, fields, lev_rows, rows), bf16),
+            jax.ShapeDtypeStruct((rows, LON), bf16),
+            jax.ShapeDtypeStruct((2 * rows, LON), bf16),
+            jax.ShapeDtypeStruct((8, 128), jnp.int32),
         ),
-        in_specs=[vmem] * 6,
-        out_specs=(vmem, vmem),
+        in_specs=[vmem] + [hbm] * 6,
+        out_specs=(vmem,) * 4,
         scratch_shapes=[
-            pltpu.VMEM((groups, lev_rows, columns), jnp.bfloat16),
-            pltpu.VMEM((everyone, message, width), jnp.bfloat16),
-            pltpu.VMEM((everyone, message, width), jnp.bfloat16),
-            pltpu.VMEM((everyone * message, width), jnp.float32),
-            pltpu.VMEM((used * halo_rows, rows), jnp.float32),
+            pltpu.VMEM((modes, modes), bf16),
+            pltpu.VMEM((modes, modes), bf16),
+            pltpu.VMEM((1, modes), jnp.float32),
+            pltpu.VMEM((part_slots, lat_total, degrees), bf16),
+            pltpu.VMEM((1, shards * slots), jnp.int32),
+            pltpu.VMEM((1, lat_rows), jnp.int32),
+            pltpu.VMEM((groups, lev_rows, columns), bf16),
+            pltpu.VMEM((groups, lev_rows, columns), bf16),
+            pltpu.VMEM((everyone, message, rows), bf16),
+            pltpu.VMEM((everyone, message, rows), bf16),
+            pltpu.VMEM((everyone * message, rows), jnp.float32),
+            pltpu.SemaphoreType.DMA((6,)),
             pltpu.SemaphoreType.DMA((2,)),
             pltpu.SemaphoreType.DMA((groups,)),
             pltpu.SemaphoreType.DMA((groups,)),
@@ -350,24 +389,25 @@
         ),
         name="exchange",
     )(
-        x, modes_in, modes_out, mode_depth.reshape(1, -1),
-        jnp.swapaxes(legendre, 1, 2), wave_map.reshape(1, -1),
+        x, modes_in, modes_out, mode_depth.reshape(1, -1), jnp.swapaxes(legendre, 1, 2),
+        wave_map.reshape(1, -1), row_points.reshape(1, -1),
     )
-    chunk = 8
+    chunk = 16
     return pl.pallas_call(
         functools.partial(section_kernel, None if exact else norm),
         grid=(lev_rows // chunk,),
         out_shape=jax.ShapeDtypeStruct((fields, lev_rows, lat_rows, LON), jnp.float32),
         in_specs=[
-            pl.BlockSpec(memory_space=pltpu.SMEM),
-            pl.BlockSpec((fields, chunk, halo_rows, rows), lambda i: (0, i, 0, 0)),
+            pl.BlockSpec((8, 128), lambda i: (0, 0)),
+            pl.BlockSpec((halo_rows, fields, chunk, rows), lambda i: (0, 0, i, 0)),
             pl.BlockSpec((rows, LON), lambda i: (0, 0)),
+            pl.BlockSpec((2 * rows, LON), lambda i: (0, 0)),
         ],
         out_specs=pl.BlockSpec((fields, chunk, lat_rows, LON), lambda i: (0, i, 0, 0)),
-        scratch_shapes=[pltpu.VMEM((fields, chunk, halo_rows, LON), jnp.float32)],
-        compiler_params=pltpu.CompilerParams(vmem_limit_bytes=32 * 1024 * 1024),
+        scratch_shapes=[pltpu.VMEM((halo_rows, fields, chunk, LON), jnp.float32)] * 3,
+        compiler_params=pltpu.CompilerParams(vmem_limit_bytes=48 * 1024 * 1024),
         name="sections",
-    )(row_points, bands.reshape(fields, lev_rows, halo_rows, rows), table)
+    )(limit, bands, table, slope)
 
 
 def solution(mesh):

time: 34.3 us -> 28.7 us (0.84)
  Pallas kernels: 28.2 us -> 22.7 us
    pallas_call x1, Pallas kernels: 9.95 us -> 4.58 us  [per_device(): pl.pallas_call(functools.partial(section_kernel, None if exact else norm)...]
where the time goes in v2:
time: 28.7 us; the launch traced here: 28.3 us
  Pallas kernels  22.7 us (79%)
  local copies, waits for them, and re-layouts  5.6 us (20%)
    pallas_call x1, Pallas kernels, per_device(): pl.pallas_call(functools.partial(exchange_kernel, dims), out_shape=(jax.S...  18.1 us
    pallas_call x1, Pallas kernels, per_device(): pl.pallas_call(functools.partial(section_kernel, None if exact else norm)...  4.58 us
    unnamed x12, local copies, waits for them, and re-layouts  4.31 us
    reshape x2, local copies, waits for them, and re-layouts, per_device(): x = spectral.reshape(lev_rows, groups, columns).transpose(1, 0, 2)  1.29 us

profile of v2, /device:TPU:0, one launch (start us, length us, event | category | flops | bytes accessed | tf_op | source)
XLA Modules:
  0.0 28.3 jit_solution(10777332201510607424)
XLA Ops:
  0.0 1.3 %reshape.12 = bf16[32,4,768]{2,1,0:T(4,128)(2,1)S(1)} reshape(bf16[32,8,3,2,64]{4,3,2,1,0:T(2,128)(2,1)} %param.7) | data formatting | bytes 393216 | tf_op jit(solution)/shard_map/reshape | solution.py:352
  1.3 0.0 copy-start
  1.3 0.8 %copy-done = bf16[8,64,32]{1,2,0:T(8,128)(2,1)S(1)} copy-done((bf16[8,64,32]{1,2,0:T(8,128)(2,1)S(1)}, bf16[8,64,32]{1,2,0:T(8,128)(2,1)}, u32[]{:S(2)}) %copy-start) | copy-done | bytes 32792
  2.1 0.0 copy-start.1
  2.1 0.8 %copy-done.1 = bf16[128,128]{1,0:T(8,128)(2,1)S(1)} copy-done((bf16[128,128]{1,0:T(8,128)(2,1)S(1)}, bf16[128,128]{1,0:T(8,128)(2,1)}, u32[]{:S(2)}) %copy-start.1) | copy-done | bytes 32792
  2.9 0.0 copy-start.2
  2.9 0.8 %copy-done.2 = bf16[128,128]{1,0:T(8,128)(2,1)S(1)} copy-done((bf16[128,128]{1,0:T(8,128)(2,1)S(1)}, bf16[128,128]{1,0:T(8,128)(2,1)}, u32[]{:S(2)}) %copy-start.2) | copy-done | bytes 32792
  3.7 0.0 copy-start.3
  3.7 0.7 %copy-done.3 = f32[128]{0:T(128)S(1)} copy-done((f32[128]{0:T(128)S(1)}, f32[128]{0:T(128)}, u32[]{:S(2)}) %copy-start.3) | copy-done | bytes 536
  4.3 0.0 copy-start.4
  4.3 0.7 %copy-done.4 = s32[64]{0:T(128)S(1)} copy-done((s32[64]{0:T(128)S(1)}, s32[64]{0:T(128)}, u32[]{:S(2)}) %copy-start.4) | copy-done | bytes 280
  5.0 0.0 copy-start.5
  5.0 0.7 %copy-done.5 = s32[4]{0:T(128)S(1)} copy-done((s32[4]{0:T(128)S(1)}, s32[4]{0:T(128)}, u32[]{:S(2)}) %copy-start.5) | copy-done | bytes 40
  5.6 18.1 %exchange.1 = (bf16[8,3,32,128]{3,2,1,0:T(8,128)(2,1)S(1)}, bf16[128,1280]{1,0:T(8,128)(2,1)S(1)}, bf16[256,1280]{1,0:T(8,128)(2,1)S(1)}, s32[8,128]{1,0:T(8,128)S(1)}) custom-call(bf16[4,32,768]{2,1,0:T(8,128)(2,1)S(1)} %bitcast.7, bf16[128,128]{1,0:T(8,128)(2,1)S(1)} %copy-done.1, bf16[128,128]{1,0:T(8,128)(2,1)S(1)} %copy-done.2, f32[1,128]{1,0:T(1,128)S(1)} %bitcast.9, ...), custom_call_target="tpu_custom_call" | custom-call | tf_op jit(solution)/shard_map/exchange/pallas_call | solution.py:358
  23.7 4.6 %sections.1 = f32[3,32,4,1280]{3,2,1,0:T(4,128)} custom-call(s32[8,128]{1,0:T(8,128)S(1)} %get-tuple-element.9.limit_ref, bf16[8,3,32,128]{3,2,1,0:T(8,128)(2,1)S(1)} %get-tuple-element.10.bands_ref, bf16[128,1280]{1,0:T(8,128)(2,1)S(1)} %get-tuple-element.11.table_ref, bf16[256,1280]{1,0:T(8,128)(2,1)S(1)} %get-tuple-element.12.slope_ref), custom_call_target="tpu_custom_call" | custom-call | tf_op jit(solution)/shard_map/sections/pallas_call | solution.py:396
  (1 shorter events, 0.0 us)
Async XLA Ops:
  1.3 0.8 %copy-start = (bf16[8,64,32]{1,2,0:T(8,128)(2,1)S(1)}, bf16[8,64,32]{1,2,0:T(8,128)(2,1)}, u32[]{:S(2)}) copy-start(bf16[8,64,32]{1,2,0:T(8,128)(2,1)} %param.11) | copy-start | bytes 98308
  2.1 0.8 %copy-start.1 = (bf16[128,128]{1,0:T(8,128)(2,1)S(1)}, bf16[128,128]{1,0:T(8,128)(2,1)}, u32[]{:S(2)}) copy-start(bf16[128,128]{1,0:T(8,128)(2,1)} %min_hbm.1) | copy-start | bytes 98308
  2.9 0.8 %copy-start.2 = (bf16[128,128]{1,0:T(8,128)(2,1)S(1)}, bf16[128,128]{1,0:T(8,128)(2,1)}, u32[]{:S(2)}) copy-start(bf16[128,128]{1,0:T(8,128)(2,1)} %mout_hbm.1) | copy-start | bytes 98308
  3.7 0.7 %copy-start.3 = (f32[128]{0:T(128)S(1)}, f32[128]{0:T(128)}, u32[]{:S(2)}) copy-start(f32[128]{0:T(128)} %param.10) | copy-start | bytes 1540
  4.3 0.7 %copy-start.4 = (s32[64]{0:T(128)S(1)}, s32[64]{0:T(128)}, u32[]{:S(2)}) copy-start(s32[64]{0:T(128)} %param.12) | copy-start | bytes 772
  5.0 0.7 %copy-start.5 = (s32[4]{0:T(128)S(1)}, s32[4]{0:T(128)}, u32[]{:S(2)}) copy-start(s32[4]{0:T(128)} %param.13) | copy-start | bytes 52

commit v3 on v2

--- a/solution.py
+++ b/solution.py
@@ -115,10 +115,10 @@
 
 def exchange_kernel(
     dims, x_ref, min_hbm, mout_hbm, depth_hbm, leg_hbm, wm_hbm, points_hbm,
-    bands_ref, table_ref, slope_ref, limit_ref,
-    min_ref, mout_ref, depth_ref, leg_ref, wm_ref, points_ref,
+    bands_ref, table_hbm, slope_hbm, limit_hbm,
+    table_ref, slope_ref, limit_ref, min_ref, mout_ref, depth_ref, leg_ref, wm_ref, points_ref,
     levels_buf, solved_buf, send_buf, recv_buf, wide,
-    in_sem, own_sem, lev_send, lev_recv, all_send, all_recv,
+    in_sem, out_sem, own_sem, lev_send, lev_recv, all_send, all_recv,
 ):
     groups, shards, slots, lev_rows, fields, degrees, lat_total, scale = dims
     halo_rows = 8
@@ -209,6 +209,10 @@
     match = iota((limit_ref.shape[0], lat_rows), 0) == iota((limit_ref.shape[0], lat_rows), 1)
     limit = jnp.sum(jnp.where(match, points_ref[...].astype(jnp.float32), 0.0), axis=1, keepdims=True)
     limit_ref[...] = jnp.broadcast_to(limit, limit_ref.shape).astype(jnp.int32)
+    pairs = [(table_ref, table_hbm), (slope_ref, slope_hbm), (limit_ref, limit_hbm)]
+    outputs = [pltpu.make_async_copy(a, b, out_sem.at[i]) for i, (a, b) in enumerate(pairs)]
+    for copy in outputs:
+        copy.start()
 
     own.wait()
     for step in range(1, groups):
@@ -298,6 +302,8 @@
     lax.fori_loop(1, everyone, sent, 0)
     for step in range(1, groups):
         lev_copy(step).wait_send()
+    for copy in outputs:
+        copy.wait()
 
 
 def section_kernel(scale, limit_ref, bands_ref, table_ref, slope_ref, out_ref, grid_buf, lon_buf, first_buf):
@@ -363,9 +369,12 @@
             jax.ShapeDtypeStruct((2 * rows, LON), bf16),
             jax.ShapeDtypeStruct((8, 128), jnp.int32),
         ),
-        in_specs=[vmem] + [hbm] * 6,
-        out_specs=(vmem,) * 4,
+        in_specs=[hbm] * 7,
+        out_specs=(vmem, hbm, hbm, hbm),
         scratch_shapes=[
+            pltpu.VMEM((rows, LON), bf16),
+            pltpu.VMEM((2 * rows, LON), bf16),
+            pltpu.VMEM((8, 128), jnp.int32),
             pltpu.VMEM((modes, modes), bf16),
             pltpu.VMEM((modes, modes), bf16),
             pltpu.VMEM((1, modes), jnp.float32),
@@ -378,6 +387,7 @@
             pltpu.VMEM((everyone, message, rows), bf16),
             pltpu.VMEM((everyone * message, rows), jnp.float32),
             pltpu.SemaphoreType.DMA((6,)),
+            pltpu.SemaphoreType.DMA((3,)),
             pltpu.SemaphoreType.DMA((2,)),
             pltpu.SemaphoreType.DMA((groups,)),
             pltpu.SemaphoreType.DMA((groups,)),
@@ -385,7 +395,7 @@
             pltpu.SemaphoreType.DMA((everyone,)),
         ],
         compiler_params=pltpu.CompilerParams(
-            collective_id=0, has_side_effects=True, vmem_limit_bytes=32 * 1024 * 1024
+            collective_id=0, has_side_effects=True, vmem_limit_bytes=60 * 1024 * 1024
         ),
         name="exchange",
     )(
@@ -405,7 +415,7 @@
         ],
         out_specs=pl.BlockSpec((fields, chunk, lat_rows, LON), lambda i: (0, i, 0, 0)),
         scratch_shapes=[pltpu.VMEM((halo_rows, fields, chunk, LON), jnp.float32)] * 3,
-        compiler_params=pltpu.CompilerParams(vmem_limit_bytes=48 * 1024 * 1024),
+        compiler_params=pltpu.CompilerParams(vmem_limit_bytes=60 * 1024 * 1024),
         name="sections",
     )(limit, bands, table, slope)
 

time: 28.7 us -> 27 us (0.941)
  local copies, waits for them, and re-layouts: 5.6 us -> 1.96 us
  Pallas kernels: 22.7 us -> 24.8 us
    unnamed x12 -> x0, local copies, waits for them, and re-layouts: 4.31 us -> none
    pallas_call x1, Pallas kernels: 4.58 us -> 5.81 us  [per_device(): pl.pallas_call(functools.partial(section_kernel, None if exact else norm)...]
    pallas_call x1, Pallas kernels: 18.1 us -> 19 us  [per_device(): pl.pallas_call(functools.partial(exchange_kernel, dims), out_shape=(jax.S...]
    reshape x2, local copies, waits for them, and re-layouts: 1.29 us -> 1.96 us  [per_device(): x = spectral.reshape(lev_rows, groups, columns).transpose(1, 0, 2)]
where the time goes in v3:
time: 27 us; the launch traced here: 26.8 us
  Pallas kernels  24.8 us (92%)
  local copies, waits for them, and re-layouts  1.96 us (7%)
    pallas_call x1, Pallas kernels, per_device(): pl.pallas_call(functools.partial(exchange_kernel, dims), out_shape=(jax.S...  19 us
    pallas_call x1, Pallas kernels, per_device(): pl.pallas_call(functools.partial(section_kernel, None if exact else norm)...  5.81 us
    reshape x2, local copies, waits for them, and re-layouts, per_device(): x = spectral.reshape(lev_rows, groups, columns).transpose(1, 0, 2)  1.96 us

profile of v3, /device:TPU:0, one launch (start us, length us, event | category | flops | bytes accessed | tf_op | source)
XLA Modules:
  0.0 26.8 jit_solution(17638600473322370825)
XLA Ops:
  0.0 1.3 %reshape.12 = bf16[32,4,768]{2,1,0:T(4,128)(2,1)S(1)} reshape(bf16[32,8,3,2,64]{4,3,2,1,0:T(2,128)(2,1)} %param.7) | data formatting | bytes 393216 | tf_op jit(solution)/shard_map/reshape | solution.py:358
  1.3 0.7 %copy.10 = bf16[32,4,768]{2,0,1:T(8,128)(2,1)} copy(bf16[32,4,768]{2,1,0:T(4,128)(2,1)S(1)} %reshape.12) | data formatting | bytes 393216 | tf_op jit(solution)/shard_map/reshape | solution.py:358
  2.0 19.0 %exchange.1 = (bf16[8,3,32,128]{3,2,1,0:T(8,128)(2,1)}, bf16[128,1280]{1,0:T(8,128)(2,1)}, bf16[256,1280]{1,0:T(8,128)(2,1)}, s32[8,128]{1,0:T(8,128)}) custom-call(bf16[4,32,768]{2,1,0:T(8,128)(2,1)} %bitcast.7, bf16[128,128]{1,0:T(8,128)(2,1)} %min_hbm.1, bf16[128,128]{1,0:T(8,128)(2,1)} %mout_hbm.1, f32[1,128]{1,0:T(1,128)} %bitcast.9, ...), custom_call_target="tpu_custom_call" | custom-call | tf_op jit(solution)/shard_map/exchange/pallas_call | solution.py:364
  21.0 5.8 %sections.1 = f32[3,32,4,1280]{3,2,1,0:T(4,128)} custom-call(s32[8,128]{1,0:T(8,128)} %get-tuple-element.9.limit_ref, bf16[8,3,32,128]{3,2,1,0:T(8,128)(2,1)} %get-tuple-element.10.bands_ref, bf16[128,1280]{1,0:T(8,128)(2,1)} %get-tuple-element.11.table_ref, bf16[256,1280]{1,0:T(8,128)(2,1)} %get-tuple-element.12.slope_ref), custom_call_target="tpu_custom_call" | custom-call | tf_op jit(solution)/shard_map/sections/pallas_call | solution.py:406

commit v4 on v3

--- a/solution.py
+++ b/solution.py
@@ -148,21 +148,14 @@
     inputs = [pltpu.make_async_copy(a, b, in_sem.at[i]) for i, (a, b) in enumerate(pairs)]
     for copy in inputs:
         copy.start()
-    own = pltpu.make_async_copy(x_ref.at[q], levels_buf.at[q], own_sem.at[0])
+    columns = levels_buf.shape[2]
+
+    def part_of(peer):
+        return x_ref.at[:, pl.ds(pl.multiple_of(peer * columns, 128), columns)]
+
+    own = pltpu.make_async_copy(part_of(q), levels_buf.at[q], own_sem.at[0])
     own.start()
 
-    pl.semaphore_wait(barrier, everyone - 1)
-
-    def lev_copy(step):
-        peer = lax.rem(q + step, groups)
-        return pltpu.make_async_remote_copy(
-            src_ref=x_ref.at[peer], dst_ref=levels_buf.at[q],
-            send_sem=lev_send.at[peer], recv_sem=lev_recv.at[q],
-            device_id=(peer, w), device_id_type=pl.DeviceIdType.MESH,
-        )
-
-    for step in range(1, groups):
-        lev_copy(step).start()
     for copy in inputs:
         copy.wait()
 
@@ -193,37 +186,27 @@
     ratio = degree_row * (degree_row + 1.0) / float(degrees * degrees)
     damp = 1.0 / (1.0 + depth * ratio)
 
-    rows = 2 * total_slots
-    row = iota((rows, total_slots), 0)
-    slot = part_slots * (row % everyone) + row // (2 * everyone)
-    waves = jnp.sum(jnp.where(slot == iota((rows, total_slots), 1), wm, 0.0), axis=1, keepdims=True)
-    parts = ((iota((rows, 1), 0) // everyone) % 2).astype(jnp.float32)
-    points = table_ref.shape[1]
-    table = (trig_rows_of(waves, parts, points) * scale).astype(jnp.bfloat16)
-    table_ref[...] = table
-    table = table.astype(jnp.float32)
-    slope = pltpu.roll(table, points - 1, 1) - pltpu.roll(table, 1, 1)
-    high = slope.astype(jnp.bfloat16)
-    slope_ref[:rows] = high
-    slope_ref[rows:] = (slope - high.astype(jnp.float32)).astype(jnp.bfloat16)
-    match = iota((limit_ref.shape[0], lat_rows), 0) == iota((limit_ref.shape[0], lat_rows), 1)
-    limit = jnp.sum(jnp.where(match, points_ref[...].astype(jnp.float32), 0.0), axis=1, keepdims=True)
-    limit_ref[...] = jnp.broadcast_to(limit, limit_ref.shape).astype(jnp.int32)
-    pairs = [(table_ref, table_hbm), (slope_ref, slope_hbm), (limit_ref, limit_hbm)]
-    outputs = [pltpu.make_async_copy(a, b, out_sem.at[i]) for i, (a, b) in enumerate(pairs)]
-    for copy in outputs:
-        copy.start()
-
+    pl.semaphore_wait(barrier, everyone - 1)
+
+    def lev_copy(step):
+        peer = lax.rem(q + step, groups)
+        return pltpu.make_async_remote_copy(
+            src_ref=part_of(peer), dst_ref=levels_buf.at[q],
+            send_sem=lev_send.at[peer], recv_sem=lev_recv.at[q],
+            device_id=(peer, w), device_id_type=pl.DeviceIdType.MESH,
+        )
+
+    for step in range(1, groups):
+        lev_copy(step).start()
     own.wait()
     for step in range(1, groups):
         peer = lax.rem(q + step, groups)
         pltpu.make_async_remote_copy(
-            src_ref=x_ref.at[peer], dst_ref=levels_buf.at[peer],
+            src_ref=part_of(peer), dst_ref=levels_buf.at[peer],
             send_sem=lev_send.at[peer], recv_sem=lev_recv.at[peer],
             device_id=(peer, w), device_id_type=pl.DeviceIdType.MESH,
         ).wait_recv()
 
-    columns = levels_buf.shape[2]
     level_count = groups * lev_rows
     coef = levels_buf[...].reshape(level_count, columns)
     modal = jnp.dot(min_ref[...], coef, preferred_element_type=jnp.float32)
@@ -268,6 +251,27 @@
             return carry
 
         lax.fori_loop(0 if turn < groups - 1 else 1, shards, start, 0)
+    rows = 2 * total_slots
+    row = iota((rows, total_slots), 0)
+    slot = part_slots * (row % everyone) + row // (2 * everyone)
+    waves = jnp.sum(jnp.where(slot == iota((rows, total_slots), 1), wm, 0.0), axis=1, keepdims=True)
+    parts = ((iota((rows, 1), 0) // everyone) % 2).astype(jnp.float32)
+    points = table_ref.shape[1]
+    table = (trig_rows_of(waves, parts, points) * scale).astype(jnp.bfloat16)
+    table_ref[...] = table
+    table = table.astype(jnp.float32)
+    slope = pltpu.roll(table, points - 1, 1) - pltpu.roll(table, 1, 1)
+    high = slope.astype(jnp.bfloat16)
+    slope_ref[:rows] = high
+    slope_ref[rows:] = (slope - high.astype(jnp.float32)).astype(jnp.bfloat16)
+    match = iota((limit_ref.shape[0], lat_rows), 0) == iota((limit_ref.shape[0], lat_rows), 1)
+    limit = jnp.sum(jnp.where(match, points_ref[...].astype(jnp.float32), 0.0), axis=1, keepdims=True)
+    limit_ref[...] = jnp.broadcast_to(limit, limit_ref.shape).astype(jnp.int32)
+    pairs = [(table_ref, table_hbm), (slope_ref, slope_hbm), (limit_ref, limit_hbm)]
+    outputs = [pltpu.make_async_copy(a, b, out_sem.at[i]) for i, (a, b) in enumerate(pairs)]
+    for copy in outputs:
+        copy.start()
+
     mine = pltpu.make_async_copy(send_buf.at[me], recv_buf.at[me], own_sem.at[1])
     mine.start()
     mine.wait()
@@ -355,7 +359,7 @@
     exact = math.frexp(norm)[0] == 0.5
     columns = part_slots * fields * 2 * degrees
     modes = modes_in.shape[0]
-    x = spectral.reshape(lev_rows, groups, columns).transpose(1, 0, 2)
+    x = spectral.reshape(lev_rows, groups * columns)
     dims = (groups, shards, slots, lev_rows, fields, degrees, lat_total, norm if exact else 1.0)
     vmem = pl.BlockSpec(memory_space=pltpu.VMEM)
     hbm = pl.BlockSpec(memory_space=pltpu.HBM)

time: 27 us -> 26.8 us (level)
  Pallas kernels: 24.8 us -> 24.5 us
    pallas_call x1, Pallas kernels: 19 us -> 18.7 us  [per_device(): pl.pallas_call(functools.partial(exchange_kernel, dims), out_shape=(jax.S...]
    reshape x2 -> x1, local copies, waits for them, and re-layouts: 1.96 us -> 1.99 us  [per_device(): x = spectral.reshape(lev_rows, groups * columns)]
where the time goes in v4:
time: 26.8 us; the launch traced here: 26.5 us
  Pallas kernels  24.5 us (91%)
  local copies, waits for them, and re-layouts  1.99 us (7%)
    pallas_call x1, Pallas kernels, per_device(): pl.pallas_call(functools.partial(exchange_kernel, dims), out_shape=(jax.S...  18.7 us
    pallas_call x1, Pallas kernels, per_device(): pl.pallas_call(functools.partial(section_kernel, None if exact else norm)...  5.81 us
    reshape x1, local copies, waits for them, and re-layouts, per_device(): x = spectral.reshape(lev_rows, groups * columns)  1.99 us

profile of v4, /device:TPU:0, one launch (start us, length us, event | category | flops | bytes accessed | tf_op | source)
XLA Modules:
  0.0 26.5 jit_solution(1871021604640107452)
XLA Ops:
  0.0 2.0 %reshape.12.x_ref = bf16[32,3072]{1,0:T(8,128)(2,1)} reshape(bf16[32,8,3,2,64]{4,3,2,1,0:T(2,128)(2,1)} %param.7) | data formatting | bytes 393216 | tf_op jit(solution)/shard_map/reshape | solution.py:362
  2.0 18.7 %exchange.1 = (bf16[8,3,32,128]{3,2,1,0:T(8,128)(2,1)}, bf16[128,1280]{1,0:T(8,128)(2,1)}, bf16[256,1280]{1,0:T(8,128)(2,1)}, s32[8,128]{1,0:T(8,128)}) custom-call(bf16[32,3072]{1,0:T(8,128)(2,1)} %reshape.12.x_ref, bf16[128,128]{1,0:T(8,128)(2,1)} %min_hbm.1, bf16[128,128]{1,0:T(8,128)(2,1)} %mout_hbm.1, f32[1,128]{1,0:T(1,128)} %bitcast.5, ...), custom_call_target="tpu_custom_call" | custom-call | tf_op jit(solution)/shard_map/exchange/pallas_call | solution.py:368
  20.7 5.8 %sections.1 = f32[3,32,4,1280]{3,2,1,0:T(4,128)} custom-call(s32[8,128]{1,0:T(8,128)} %get-tuple-element.9.limit_ref, bf16[8,3,32,128]{3,2,1,0:T(8,128)(2,1)} %get-tuple-element.10.bands_ref, bf16[128,1280]{1,0:T(8,128)(2,1)} %get-tuple-element.11.table_ref, bf16[256,1280]{1,0:T(8,128)(2,1)} %get-tuple-element.12.slope_ref), custom_call_target="tpu_custom_call" | custom-call | tf_op jit(solution)/shard_map/sections/pallas_call | solution.py:410

commit v5 on v4

--- a/solution.py
+++ b/solution.py
@@ -317,13 +317,11 @@
 
     def product(a, b):
         value = jnp.dot(a, b, preferred_element_type=jnp.float32)
-        return (value if scale is None else value * scale).reshape(fields, chunk, width)
-
-    for t in range(halo_rows):
-        part = bands_ref[t].reshape(fields * chunk, depth)
-        grid_buf[t] = product(part, table_ref[...])
-        if t in inner:
-            lon_buf[t] = product(jnp.concatenate([part, part], axis=1), slope_ref[...])
+        return (value if scale is None else value * scale).reshape(grid_buf.shape)
+
+    part = bands_ref[...].reshape(halo_rows * fields * chunk, depth)
+    grid_buf[...] = product(part, table_ref[...])
+    lon_buf[...] = product(jnp.concatenate([part, part], axis=1), slope_ref[...])
 
     def around(ref, t, f):
         return ref[(t + 1) % halo_rows, f] - ref[(t - 1) % halo_rows, f]

time: 26.8 us -> 26 us (0.970)
  Pallas kernels: 24.5 us -> 23.8 us
    pallas_call x1, Pallas kernels: 5.81 us -> 5.04 us  [per_device(): pl.pallas_call(functools.partial(section_kernel, None if exact else norm)...]
where the time goes in v5:
time: 26 us; the launch traced here: 25.8 us
  Pallas kernels  23.8 us (92%)
  local copies, waits for them, and re-layouts  1.99 us (8%)
    pallas_call x1, Pallas kernels, per_device(): pl.pallas_call(functools.partial(exchange_kernel, dims), out_shape=(jax.S...  18.7 us
    pallas_call x1, Pallas kernels, per_device(): pl.pallas_call(functools.partial(section_kernel, None if exact else norm)...  5.04 us
    reshape x1, local copies, waits for them, and re-layouts, per_device(): x = spectral.reshape(lev_rows, groups * columns)  1.99 us

profile of v5, /device:TPU:0, one launch (start us, length us, event | category | flops | bytes accessed | tf_op | source)
XLA Modules:
  0.0 25.8 jit_solution(14797303000809789173)
XLA Ops:
  0.0 2.0 %reshape.12.x_ref = bf16[32,3072]{1,0:T(8,128)(2,1)} reshape(bf16[32,8,3,2,64]{4,3,2,1,0:T(2,128)(2,1)} %param.7) | data formatting | bytes 393216 | tf_op jit(solution)/shard_map/reshape | solution.py:360
  2.0 18.7 %exchange.1 = (bf16[8,3,32,128]{3,2,1,0:T(8,128)(2,1)}, bf16[128,1280]{1,0:T(8,128)(2,1)}, bf16[256,1280]{1,0:T(8,128)(2,1)}, s32[8,128]{1,0:T(8,128)}) custom-call(bf16[32,3072]{1,0:T(8,128)(2,1)} %reshape.12.x_ref, bf16[128,128]{1,0:T(8,128)(2,1)} %min_hbm.1, bf16[128,128]{1,0:T(8,128)(2,1)} %mout_hbm.1, f32[1,128]{1,0:T(1,128)} %bitcast.5, ...), custom_call_target="tpu_custom_call" | custom-call | tf_op jit(solution)/shard_map/exchange/pallas_call | solution.py:366
  20.7 5.0 %sections.1 = f32[3,32,4,1280]{3,2,1,0:T(4,128)} custom-call(s32[8,128]{1,0:T(8,128)} %get-tuple-element.9.limit_ref, bf16[8,3,32,128]{3,2,1,0:T(8,128)(2,1)} %get-tuple-element.10.bands_ref, bf16[128,1280]{1,0:T(8,128)(2,1)} %get-tuple-element.11.table_ref, bf16[256,1280]{1,0:T(8,128)(2,1)} %get-tuple-element.12.slope_ref), custom_call_target="tpu_custom_call" | custom-call | tf_op jit(solution)/shard_map/sections/pallas_call | solution.py:408

commit v6 on v5

--- a/solution.py
+++ b/solution.py
@@ -404,7 +404,7 @@
         x, modes_in, modes_out, mode_depth.reshape(1, -1), jnp.swapaxes(legendre, 1, 2),
         wave_map.reshape(1, -1), row_points.reshape(1, -1),
     )
-    chunk = 16
+    chunk = 8
     return pl.pallas_call(
         functools.partial(section_kernel, None if exact else norm),
         grid=(lev_rows // chunk,),

time: 26 us -> 26.4 us (1.015)
  no operation moved by 1% of the time
where the time goes in v6:
time: 26.4 us; the launch traced here: 26 us
  Pallas kernels  24 us (91%)
  local copies, waits for them, and re-layouts  1.99 us (8%)
    pallas_call x1, Pallas kernels, per_device(): pl.pallas_call(functools.partial(exchange_kernel, dims), out_shape=(jax.S...  18.7 us
    pallas_call x1, Pallas kernels, per_device(): pl.pallas_call(functools.partial(section_kernel, None if exact else norm)...  5.26 us
    reshape x1, local copies, waits for them, and re-layouts, per_device(): x = spectral.reshape(lev_rows, groups * columns)  1.99 us

profile of v6, /device:TPU:0, one launch (start us, length us, event | category | flops | bytes accessed | tf_op | source)
XLA Modules:
  0.0 26.0 jit_solution(13137948635069601849)
XLA Ops:
  0.0 2.0 %reshape.12.x_ref = bf16[32,3072]{1,0:T(8,128)(2,1)} reshape(bf16[32,8,3,2,64]{4,3,2,1,0:T(2,128)(2,1)} %param.7) | data formatting | bytes 393216 | tf_op jit(solution)/shard_map/reshape | solution.py:360
  2.0 18.7 %exchange.1 = (bf16[8,3,32,128]{3,2,1,0:T(8,128)(2,1)}, bf16[128,1280]{1,0:T(8,128)(2,1)}, bf16[256,1280]{1,0:T(8,128)(2,1)}, s32[8,128]{1,0:T(8,128)}) custom-call(bf16[32,3072]{1,0:T(8,128)(2,1)} %reshape.12.x_ref, bf16[128,128]{1,0:T(8,128)(2,1)} %min_hbm.1, bf16[128,128]{1,0:T(8,128)(2,1)} %mout_hbm.1, f32[1,128]{1,0:T(1,128)} %bitcast.5, ...), custom_call_target="tpu_custom_call" | custom-call | tf_op jit(solution)/shard_map/exchange/pallas_call | solution.py:366
  20.7 5.3 %sections.1 = f32[3,32,4,1280]{3,2,1,0:T(4,128)} custom-call(s32[8,128]{1,0:T(8,128)} %get-tuple-element.9.limit_ref, bf16[8,3,32,128]{3,2,1,0:T(8,128)(2,1)} %get-tuple-element.10.bands_ref, bf16[128,1280]{1,0:T(8,128)(2,1)} %get-tuple-element.11.table_ref, bf16[256,1280]{1,0:T(8,128)(2,1)} %get-tuple-element.12.slope_ref), custom_call_target="tpu_custom_call" | custom-call | tf_op jit(solution)/shard_map/sections/pallas_call | solution.py:408
